TPU v7x, 32 devices: a whole 2x2x4 slice. The times are simulated.
32 devices in a mesh: groups: 2 (over y), row: 4 (over x, core), col: 4 (over z).
Axes of the slice: x: 2, y: 2, z: 4, core: 2. Of those that a mesh axis runs over, the one named last changes fastest.
Arguments:
- inputs: bfloat16 [256, 6144], P(('groups', 'row'), 'col'), parts along dimension 0, may hold values from -6 to 6
- upstream: bfloat16 [256, 6144], P(('groups', 'row'), 'col'), parts along dimension 0, may hold values from -6 to 6
- weight_in: bfloat16 [6144, 24576], P('col', 'row'), may hold values from -0.078125 to 0.078125
- weight_out: bfloat16 [24576, 6144], P('row', 'col'), may hold values from -0.0390625 to 0.0390625
Outputs:
- result: bfloat16 [256, 6144], P(('groups', 'row'), 'col'), parts along dimension 0
- grad_inputs: bfloat16 [256, 6144], P(('groups', 'row'), 'col'), parts along dimension 0
- grad_weight_in: bfloat16 [12288, 24576], P(('groups', 'col'), 'row'), parts along dimension 0
- grad_weight_out: bfloat16 [49152, 6144], P(('groups', 'row'), 'col'), parts along dimension 0
There are 2 independent parts, one for each index of `groups`. A program takes and returns all parts, laid end to end along the dimension named above; an argument that names none is the same for every part. Nothing has to cross between parts.
All inputs are finite; a program needn't handle non-finite values.
Results may differ from a plain program's by a relative error of at most 0.0051.
Values may be sent and summed in bfloat16 or wider, within the bound.
A program may use at most 192 MiB of HBM per device.

v0:
```python
import math

import jax
import jax.numpy as jnp
from jax import lax
from jax.sharding import PartitionSpec as P

gelu_c = math.sqrt(2.0 / math.pi)


def local_gelu(preact, grad_act):
    inner = gelu_c * (preact + 0.044715 * preact * preact * preact)
    tangent = jnp.tanh(inner)
    value = 0.5 * preact * (1.0 + tangent)
    slope = 0.5 * (1.0 + tangent) + 0.5 * preact * (1.0 - tangent * tangent) * gelu_c * (
        1.0 + 3.0 * 0.044715 * preact * preact
    )
    return (value.astype(jnp.bfloat16), (grad_act * slope).astype(jnp.bfloat16))


def shards(inputs, upstream, weight_in, weight_out):
    gathered_x, gathered_dy = (
        lax.all_gather(inputs, "row", axis=0, tiled=True),
        lax.all_gather(upstream, "row", axis=0, tiled=True),
    )
    part_pre = jnp.dot(gathered_x, weight_in, preferred_element_type=jnp.float32)
    part_grad = lax.dot_general(
        gathered_dy, weight_out, (((1,), (1,)), ((), ())), preferred_element_type=jnp.float32
    )
    preact, grad_act = lax.psum((part_pre, part_grad), "col")
    activation, grad_pre = local_gelu(preact, grad_act)
    part_out = jnp.dot(activation, weight_out, preferred_element_type=jnp.float32)
    part_back = lax.dot_general(
        grad_pre, weight_in, (((1,), (1,)), ((), ())), preferred_element_type=jnp.float32
    )
    grad_weight_out = lax.dot_general(
        activation, gathered_dy, (((0,), (0,)), ((), ())), preferred_element_type=jnp.float32
    ).astype(jnp.bfloat16)
    grad_weight_in = lax.dot_general(
        gathered_x, grad_pre, (((0,), (0,)), ((), ())), preferred_element_type=jnp.float32
    ).astype(jnp.bfloat16)
    summed_out, summed_back = (
        lax.psum_scatter(part_out, "row", scatter_dimension=0, tiled=True),
        lax.psum_scatter(part_back, "row", scatter_dimension=0, tiled=True),
    )
    return (
        summed_out.astype(jnp.bfloat16),
        summed_back.astype(jnp.bfloat16),
        grad_weight_in,
        grad_weight_out,
    )


def solution(mesh):
    placed = (
        P(("groups", "row"), "col"),
        P(("groups", "row"), "col"),
        P("col", "row"),
        P("row", "col"),
    )
    return jax.shard_map(
        shards,
        mesh=mesh,
        in_specs=placed,
        out_specs=(
            P(("groups", "row"), "col"),
            P(("groups", "row"), "col"),
            P(("groups", "col"), "row"),
            P(("groups", "row"), "col"),
        ),
        check_vma=False,
    )
```

profile of v0, /device:TPU:1, one launch (start us, length us, event | category | flops | bytes accessed | tf_op | source)
XLA Modules:
  0.0 355.9 jit_solution(838352096428845371)
XLA Ops:
  7.2 0.0 all-reduce.3.cloned.1.call-start
  7.2 8.0 %all_gather.6 = bf16[128,1536]{1,0:T(8,128)(2,1)S(1)} all-gather(bf16[32,1536]{1,0:T(8,128)(2,1)} %param.4), channel_id=1, replica_groups=mesh['groups'=2,'row'=4,'col'=4] {'row'}, dimensions={0}, use_global_device_ids=true | all-gather | bytes 491520 | tf_op jit(solution)/shard_map/all_gather | solution.py:23
  15.2 0.0 copy-start.1
  15.2 6.8 %all_gather.7 = bf16[128,1536]{1,0:T(8,128)(2,1)S(1)} all-gather(bf16[32,1536]{1,0:T(8,128)(2,1)} %param.5), channel_id=1, replica_groups=mesh['groups'=2,'row'=4,'col'=4] {'row'}, dimensions={0}, use_global_device_ids=true | all-gather | bytes 491520 | tf_op jit(solution)/shard_map/all_gather | solution.py:24
  22.0 0.0 copy-done.1
  22.0 11.0 %fusion.9 = f32[128,6144]{1,0:T(8,128)} fusion(bf16[128,1536]{1,0:T(8,128)(2,1)S(1)} %all_gather.6, bf16[1536,6144]{1,0:T(8,128)(2,1)} %param.6), kind=kOutput, calls=%fused_computation.14 | convolution fusion | flops 2415919104 | bytes 22413312 | tf_op jit(solution)/shard_map/dot_general | solution.py:26
  33.0 14.0 %fusion.10 = f32[128,6144]{1,0:T(8,128)} fusion(bf16[128,1536]{1,0:T(8,128)(2,1)S(1)} %all_gather.7, bf16[6144,1536]{1,0:T(8,128)(2,1)} %param.7), kind=kOutput, calls=%fused_computation.15 | convolution fusion | flops 2415919104 | bytes 22413312 | tf_op jit(solution)/shard_map/dot_general | solution.py:27
  47.0 0.0 all-reduce.3.cloned.1.call-update
  47.1 0.0 reduce-scatter.3.cloned.1.call-start
  47.1 223.9 %all-reduce.3.cloned.1.call-done = (f32[128,6144]{1,0:T(8,128)}, f32[128,6144]{1,0:T(8,128)}) async-done(((f32[128,6144]{1,0:T(8,128)}, f32[128,6144]{1,0:T(8,128)}), (f32[128,6144]{1,0:T(8,128)}, f32[128,6144]{1,0:T(8,128)})) %all-reduce.3.cloned.1.call-update) | async-done | bytes 6291472 | tf_op jit(solution)/shard_map/psum | solution.py:30
  271.0 0.0 copy-start
  271.0 11.3 %fusion.8 = f32[128,1536]{1,0:T(8,128)} fusion(bf16[6144,1536]{1,0:T(8,128)(2,1)} %param.7, f32[128,6144]{1,0:T(8,128)} %get-tuple-element.8), kind=kOutput, calls=%fused_computation.13 | convolution fusion | flops 2422996992 | bytes 22806528 | tf_op jit(solution)/shard_map/dot_general | solution.py:32
  282.3 0.0 reduce-scatter.3.cloned.1.call-update
  282.4 0.2 reduce-scatter.5.cloned.1.call-start
  282.6 0.0 copy-done
  282.6 4.3 %fusion.7 = bf16[128,6144]{1,0:T(8,128)(2,1)} fusion(f32[128,6144]{1,0:T(8,128)} %get-tuple-element.9, f32[128,6144]{1,0:T(8,128)S(1)} %copy-done), kind=kLoop, calls=%fused_computation.11 | loop fusion | flops 14942208 | bytes 7864320 | tf_op jit(solution)/shard_map/convert_element_type | solution.py:18
  286.9 14.4 %fusion.11 = f32[128,1536]{1,0:T(8,128)} fusion(bf16[128,6144]{1,0:T(8,128)(2,1)} %fusion.7, bf16[1536,6144]{1,0:T(8,128)(2,1)} %param.6), kind=kOutput, calls=%fused_computation.16 | convolution fusion | flops 2415919104 | bytes 21233664 | tf_op jit(solution)/shard_map/dot_general | solution.py:33
  301.3 0.0 reduce-scatter.5.cloned.1.call-update
  301.3 10.7 %fusion = bf16[1536,6144]{0,1:T(8,128)(2,1)} fusion(bf16[128,6144]{1,0:T(8,128)(2,1)} %fusion.7, bf16[128,1536]{1,0:T(8,128)(2,1)} %copy-done.1), kind=kOutput, calls=%fused_computation.2 | convolution fusion | flops 2425356288 | bytes 20840448 | tf_op jit(solution)/shard_map/dot_general | solution.py:39
  312.0 24.7 %copy.8 = bf16[1536,6144]{1,0:T(8,128)(2,1)} copy(bf16[1536,6144]{0,1:T(8,128)(2,1)} %fusion) | data formatting | bytes 37748736
  336.7 9.5 %convolution_convert_fusion = bf16[6144,1536]{1,0:T(8,128)(2,1)} fusion(bf16[128,1536]{1,0:T(8,128)(2,1)S(1)} %all_gather.7, f32[128,6144]{1,0:T(8,128)S(1)} %copy-done), kind=kOutput, calls=%fused_computation | convolution fusion | flops 2432434176 | bytes 22413312 | tf_op jit(solution)/shard_map/dot_general | solution.py:36
  346.2 0.0 reduce-scatter.3.cloned.1.call-done
  346.2 1.6 convert_element_type.22
  347.8 0.0 reduce-scatter.5.cloned.1.call-done
  347.8 1.6 convert_element_type.24
Async XLA Ops:
  7.2 263.8 %all-reduce.3.cloned.1.call-start = ((), (), s32[]{:S(2)}) async-start(), calls=%async_computation.4 | async-start | bytes 12582912 | tf_op jit(solution)/shard_map/psum | solution.py:30
  15.2 6.8 %copy-start.1 = (bf16[128,1536]{1,0:T(8,128)(2,1)}, bf16[128,1536]{1,0:T(8,128)(2,1)S(1)}, u32[]{:S(2)}) copy-start(bf16[128,1536]{1,0:T(8,128)(2,1)S(1)} %all_gather.6) | copy-start | bytes 1179652
  47.1 299.2 %reduce-scatter.3.cloned.1.call-start = ((), (), s32[]{:S(2)}) async-start(), calls=%async_computation.2 | async-start | bytes 983040 | tf_op jit(solution)/shard_map/reduce_scatter | solution.py:43
  271.0 11.6 %copy-start = (f32[128,6144]{1,0:T(8,128)S(1)}, f32[128,6144]{1,0:T(8,128)}, u32[]{:S(2)}) copy-start(f32[128,6144]{1,0:T(8,128)} %get-tuple-element.8) | copy-start | bytes 9437188
  282.4 65.5 %reduce-scatter.5.cloned.1.call-start = ((), (), s32[]{:S(2)}) async-start(), calls=%async_computation.3 | async-start | bytes 983040 | tf_op jit(solution)/shard_map/reduce_scatter | solution.py:44
Sparse Core Ops, SparseCore 0:
  47.2 223.7 all-reduce.2
  282.5 22.1 reduce-scatter.2
  307.4 23.2 reduce-scatter.4
where the time goes:
time: 357 us; the launch traced here: 356 us
  waiting for transfers between devices  224 us (63%)
  matrix products  71 us (20%)
  local copies, waits for them, and re-layouts  24.7 us (7%)
  blocking collectives  14.8 us (4%)
  between operations  13.8 us (4%)
  other arithmetic  7.45 us (2%)
    psum x1, waiting for transfers between devices, shards(): preact, grad_act = lax.psum((part_pre, part_grad), 'col')  224 us
    unnamed x5, local copies, waits for them, and re-layouts  24.7 us
    dot_general x1, matrix products, shards(): lax.dot_general(grad_pre, weight_in, (((1,), (1,)), ((), ())), preferred_...  14.4 us
    dot_general x1, matrix products, shards(): lax.dot_general(gathered_dy, weight_out, (((1,), (1,)), ((), ())), prefer...  14 us
    dot_general x1, matrix products, shards(): jnp.dot(activation, weight_out, preferred_element_type=jnp.float32)  11.3 us
    dot_general x1, matrix products, shards(): jnp.dot(gathered_x, weight_in, preferred_element_type=jnp.float32)  11 us
    dot_general x1, matrix products, shards(): lax.dot_general(gathered_x, grad_pre, (((0,), (0,)), ((), ())), preferred...  10.7 us
    dot_general x1, matrix products, shards(): lax.dot_general(activation, gathered_dy, (((0,), (0,)), ((), ())), prefer...  9.52 us
  transfers between devices with their start and end apart: 3, of which 1 were waited for; matrix products, arithmetic and copies ran while one was open for 18% of the time, Pallas kernels for 0%

commit v1 on v0

v1 whole, which is shorter than its diff:
```python
import functools
import math

import jax
import jax.numpy as jnp
from jax import lax
from jax.experimental import pallas as pl
from jax.experimental.pallas import tpu as pltpu
from jax.sharding import PartitionSpec as P

gelu_c = math.sqrt(2.0 / math.pi)
MESH = pl.DeviceIdType.MESH
CHUNK = 256
RING = 8
RELAY, OWN, SPREAD = 1, 3, 6
NT = (((1,), (1,)), ((), ()))
TN = (((0,), (0,)), ((), ()))


def local_gelu(preact, grad_act):
    inner = gelu_c * (preact + 0.044715 * preact * preact * preact)
    tangent = jnp.tanh(inner)
    value = 0.5 * preact * (1.0 + tangent)
    slope = 0.5 * (1.0 + tangent) + 0.5 * preact * (1.0 - tangent * tangent) * gelu_c * (
        1.0 + 3.0 * 0.044715 * preact * preact
    )
    return (value.astype(jnp.bfloat16), (grad_act * slope).astype(jnp.bfloat16))


def block_kernel(
    n_row, n_col, chunks,
    x_ref, dy_ref, win_hbm, wout_hbm,
    acts_hbm, xall_hbm, dyall_hbm, out_ref, back_ref,
    xall, dyall, win, wout, local, outgoing, from_left, from_right, acts,
    w_sem, g_send, g_recv, rs_send, left_recv, right_recv, ag_send, ag_recv, save_sem, tok_sem,
):
    row, col = lax.axis_index("row"), lax.axis_index("col")
    own = x_ref.shape[0]
    tokens = own * n_row
    pair, core = row // 2, row % 2
    pairs = n_row // 2
    sibling = pair * 2 + 1 - core
    mid = n_col // 2
    has_left = col > 0
    has_right = col < n_col - 1
    edge = jnp.logical_or(col == 0, col == n_col - 1)
    depth = x_ref.shape[1]

    def weight_copies(k):
        at = pl.ds(pl.multiple_of(k * CHUNK, CHUNK), CHUNK)
        return (
            pltpu.make_async_copy(win_hbm.at[:, at], win.at[k], w_sem.at[0, k]),
            pltpu.make_async_copy(wout_hbm.at[at, :], wout.at[k], w_sem.at[1, k]),
        )

    def load(k, carry):
        for copy in weight_copies(k):
            copy.start()
        return carry

    lax.fori_loop(0, chunks, load, 0)

    barrier = pltpu.get_barrier_semaphore()
    pl.semaphore_signal(barrier, inc=1, device_id={"row": sibling}, device_id_type=MESH)
    for o in range(1, pairs):
        peer = lax.rem(pair + o, pairs) * 2 + core
        pl.semaphore_signal(barrier, inc=1, device_id={"row": peer}, device_id_type=MESH)

    @pl.when(has_left)
    def _():
        pl.semaphore_signal(barrier, inc=1, device_id={"col": col - 1}, device_id_type=MESH)

    @pl.when(has_right)
    def _():
        pl.semaphore_signal(barrier, inc=1, device_id={"col": col + 1}, device_id_type=MESH)

    pl.semaphore_wait(barrier, pairs + jnp.where(edge, 1, 2))

    def token_copy(which, block, slot, peer, mine):
        ref, all_ref = ((x_ref, xall), (dy_ref, dyall))[which]
        at = pl.ds(pl.multiple_of(block * own, own), own)
        return pltpu.make_async_remote_copy(
            src_ref=ref if mine else all_ref.at[at],
            dst_ref=all_ref.at[at],
            send_sem=g_send.at[which, slot],
            recv_sem=g_recv.at[which, block],
            device_id={"row": peer},
            device_id_type=MESH,
        )

    sends = []
    for which in range(2):
        for o in range(1, pairs):
            sends.append(token_copy(which, row, o, lax.rem(pair + o, pairs) * 2 + core, True))
            sends[-1].start()
        sends.append(token_copy(which, row, 0, sibling, True))
        sends[-1].start()
    mine = pl.ds(pl.multiple_of(row * own, own), own)
    xall[mine, :] = x_ref[...]
    dyall[mine, :] = dy_ref[...]
    out_ref[...] = jnp.zeros_like(out_ref)
    back_ref[...] = jnp.zeros_like(back_ref)
    for which in range(2):
        for o in range(1, pairs):
            block = lax.rem(pair + pairs - o, pairs) * 2 + core
            onward = token_copy(which, block, pairs + o - 1, sibling, False)
            onward.wait_recv()
            onward.start()
            sends.append(onward)
    for which in range(2):
        for q in range(pairs):
            token_copy(which, q * 2 + 1 - core, 0, sibling, False).wait_recv()
    for copy in sends:
        copy.wait_send()
    keep = (
        pltpu.make_async_copy(xall, xall_hbm, tok_sem.at[0]),
        pltpu.make_async_copy(dyall, dyall_hbm, tok_sem.at[1]),
    )
    for copy in keep:
        copy.start()

    def owner(k):
        return mid - 1 + lax.rem(k, 2)

    def sum_right(k):
        return pltpu.make_async_remote_copy(
            src_ref=outgoing.at[k], dst_ref=from_left.at[k],
            send_sem=rs_send.at[k], recv_sem=left_recv.at[k],
            device_id={"col": col + 1}, device_id_type=MESH,
        )

    def sum_left(k):
        return pltpu.make_async_remote_copy(
            src_ref=outgoing.at[k], dst_ref=from_right.at[k],
            send_sem=rs_send.at[k], recv_sem=right_recv.at[k],
            device_id={"col": col - 1}, device_id_type=MESH,
        )

    def spread(k, side):
        return pltpu.make_async_remote_copy(
            src_ref=acts.at[k], dst_ref=acts.at[k],
            send_sem=ag_send.at[side, k], recv_sem=ag_recv.at[k],
            device_id={"col": col - 1 + 2 * side}, device_id_type=MESH,
        )

    def save(k):
        return pltpu.make_async_copy(acts.at[k], acts_hbm.at[k], save_sem.at[k])

    def multiply(k):
        for copy in weight_copies(k):
            copy.wait()
        slot = lax.rem(k, RING)
        pre = jnp.dot(xall[...], win[k], preferred_element_type=jnp.float32)
        grad = lax.dot_general(dyall[...], wout[k], NT, preferred_element_type=jnp.float32)

        @pl.when(edge)
        def _():
            outgoing[k, :tokens, :] = pre.astype(jnp.bfloat16)
            outgoing[k, tokens:, :] = grad.astype(jnp.bfloat16)

        @pl.when(jnp.logical_not(edge))
        def _():
            local[slot, :tokens, :] = pre
            local[slot, tokens:, :] = grad

        @pl.when(col == 0)
        def _():
            sum_right(k).start()

        @pl.when(col == n_col - 1)
        def _():
            sum_left(k).start()

    def relay(k):
        slot = lax.rem(k, RING)

        @pl.when(jnp.logical_and(has_left, col < owner(k)))
        def _():
            copy = sum_right(k)
            copy.wait_recv()
            outgoing[k] = (local[slot] + from_left[k].astype(jnp.float32)).astype(jnp.bfloat16)
            copy.start()

        @pl.when(jnp.logical_and(has_right, col > owner(k)))
        def _():
            copy = sum_left(k)
            copy.wait_recv()
            outgoing[k] = (local[slot] + from_right[k].astype(jnp.float32)).astype(jnp.bfloat16)
            copy.start()

    def activate(k):
        slot = lax.rem(k, RING)

        @pl.when(col == owner(k))
        def _():
            sum_right(k).wait_recv()
            sum_left(k).wait_recv()
            total = (
                local[slot] + from_left[k].astype(jnp.float32) + from_right[k].astype(jnp.float32)
            )
            value, slope = local_gelu(total[:tokens], total[tokens:])
            acts[k, :tokens, :] = value
            acts[k, tokens:, :] = slope
            spread(k, 0).start()
            spread(k, 1).start()

    def finish(k):
        @pl.when(col < owner(k))
        def _():
            copy = spread(k, 0)
            copy.wait_recv()

            @pl.when(has_left)
            def _():
                copy.start()

        @pl.when(col > owner(k))
        def _():
            copy = spread(k, 1)
            copy.wait_recv()

            @pl.when(has_right)
            def _():
                copy.start()

        save(k).start()
        out_ref[...] += jnp.dot(acts[k, :tokens, :], wout[k], preferred_element_type=jnp.float32)
        back_ref[...] += lax.dot_general(
            acts[k, tokens:, :], win[k], NT, preferred_element_type=jnp.float32
        )

    def step(s, carry):
        for trail, stage in ((0, multiply), (RELAY, relay), (OWN, activate), (SPREAD, finish)):
            @pl.when(jnp.logical_and(s >= trail, s < chunks + trail))
            def _():
                stage(s - trail)
        return carry

    lax.fori_loop(0, chunks + SPREAD, step, 0)

    def drain(k, carry):
        @pl.when(col < owner(k))
        def _():
            sum_right(k).wait_send()

        @pl.when(col > owner(k))
        def _():
            sum_left(k).wait_send()

        @pl.when(jnp.logical_and(has_left, col <= owner(k)))
        def _():
            spread(k, 0).wait_send()

        @pl.when(jnp.logical_and(has_right, col >= owner(k)))
        def _():
            spread(k, 1).wait_send()

        save(k).wait()
        return carry

    lax.fori_loop(0, chunks, drain, 0)
    for copy in keep:
        copy.wait()


def run_block(n_row, n_col, x, dy, w_in, w_out):
    own, depth = x.shape
    hidden = w_in.shape[1]
    chunks = hidden // CHUNK
    tokens = own * n_row
    bf, f32 = jnp.bfloat16, jnp.float32
    vmem = pl.BlockSpec(memory_space=pltpu.VMEM)
    anywhere = pl.BlockSpec(memory_space=pl.ANY)
    dma = pltpu.SemaphoreType.DMA
    stack = (chunks, 2 * tokens, CHUNK)
    return pl.pallas_call(
        functools.partial(block_kernel, n_row, n_col, chunks),
        out_shape=(
            jax.ShapeDtypeStruct(stack, bf),
            jax.ShapeDtypeStruct((tokens, depth), bf),
            jax.ShapeDtypeStruct((tokens, depth), bf),
            jax.ShapeDtypeStruct((tokens, depth), f32),
            jax.ShapeDtypeStruct((tokens, depth), f32),
        ),
        in_specs=[vmem, vmem, anywhere, anywhere],
        out_specs=(anywhere, anywhere, anywhere, vmem, vmem),
        scratch_shapes=[
            pltpu.VMEM((tokens, depth), bf),
            pltpu.VMEM((tokens, depth), bf),
            pltpu.VMEM((chunks, depth, CHUNK), bf),
            pltpu.VMEM((chunks, CHUNK, depth), bf),
            pltpu.VMEM((RING, 2 * tokens, CHUNK), f32),
            pltpu.VMEM(stack, bf),
            pltpu.VMEM(stack, bf),
            pltpu.VMEM(stack, bf),
            pltpu.VMEM(stack, bf),
            dma((2, chunks)),
            dma((2, n_row)),
            dma((2, n_row)),
            dma((chunks,)),
            dma((chunks,)),
            dma((chunks,)),
            dma((2, chunks)),
            dma((chunks,)),
            dma((chunks,)),
            dma((2,)),
        ],
        compiler_params=pltpu.CompilerParams(
            collective_id=0, has_side_effects=True, vmem_limit_bytes=60 * 2**20
        ),
        cost_estimate=pl.CostEstimate(
            flops=8 * tokens * depth * hidden,
            bytes_accessed=4 * depth * hidden,
            transcendentals=tokens * hidden,
        ),
        name="block",
    )(x, dy, w_in, w_out)


def grads_kernel(x_ref, dy_ref, acts_ref, gin_ref, gout_ref, xt):
    tokens = x_ref.shape[0]

    @pl.when(pl.program_id(0) == 0)
    def _():
        xt[...] = x_ref[...].T

    for i in range(acts_ref.shape[0]):
        at = slice(i * CHUNK, (i + 1) * CHUNK)
        gin_ref[:, at] = jnp.dot(
            xt[...], acts_ref[i, tokens:, :], preferred_element_type=jnp.float32
        ).astype(jnp.bfloat16)
        gout_ref[at, :] = lax.dot_general(
            acts_ref[i, :tokens, :], dy_ref[...], TN, preferred_element_type=jnp.float32
        ).astype(jnp.bfloat16)


def weight_grads(x, dy, acts):
    tokens, depth = x.shape
    chunks = acts.shape[0]
    hidden = chunks * CHUNK
    per = 2
    bf = jnp.bfloat16
    return pl.pallas_call(
        grads_kernel,
        grid=(chunks // per,),
        out_shape=(
            jax.ShapeDtypeStruct((depth, hidden), bf),
            jax.ShapeDtypeStruct((hidden, depth), bf),
        ),
        in_specs=[
            pl.BlockSpec((tokens, depth), lambda s: (0, 0)),
            pl.BlockSpec((tokens, depth), lambda s: (0, 0)),
            pl.BlockSpec((per, 2 * tokens, CHUNK), lambda s: (s, 0, 0)),
        ],
        out_specs=(
            pl.BlockSpec((depth, per * CHUNK), lambda s: (0, s)),
            pl.BlockSpec((per * CHUNK, depth), lambda s: (s, 0)),
        ),
        scratch_shapes=[pltpu.VMEM((depth, tokens), bf)],
        compiler_params=pltpu.CompilerParams(vmem_limit_bytes=40 * 2**20),
        cost_estimate=pl.CostEstimate(
            flops=4 * tokens * depth * hidden,
            bytes_accessed=4 * depth * hidden,
            transcendentals=0,
        ),
        name="grads",
    )(x, dy, acts)


def shards(n_row, n_col, inputs, upstream, weight_in, weight_out):
    acts, x_all, dy_all, part_out, part_back = run_block(
        n_row, n_col, inputs, upstream, weight_in, weight_out
    )
    summed_out, summed_back = (
        lax.psum_scatter(part_out, "row", scatter_dimension=0, tiled=True),
        lax.psum_scatter(part_back, "row", scatter_dimension=0, tiled=True),
    )
    grad_weight_in, grad_weight_out = weight_grads(x_all, dy_all, acts)
    return (
        summed_out.astype(jnp.bfloat16),
        summed_back.astype(jnp.bfloat16),
        grad_weight_in,
        grad_weight_out,
    )


def solution(mesh):
    placed = (
        P(("groups", "row"), "col"),
        P(("groups", "row"), "col"),
        P("col", "row"),
        P("row", "col"),
    )
    return jax.shard_map(
        functools.partial(shards, mesh.shape["row"], mesh.shape["col"]),
        mesh=mesh,
        in_specs=placed,
        out_specs=(
            P(("groups", "row"), "col"),
            P(("groups", "row"), "col"),
            P(("groups", "col"), "row"),
            P(("groups", "row"), "col"),
        ),
        check_vma=False,
    )
```

time: 357 us -> 183 us (0.51)
  waiting for transfers between devices: 224 us -> 32.9 us
  Pallas kernels: 0 us -> 128 us
  matrix products: 71 us -> 0 us
  local copies, waits for them, and re-layouts: 24.7 us -> 3.87 us
  blocking collectives: 14.8 us -> 0 us
  other arithmetic: 7.45 us -> 3.15 us
    psum x1 -> x0, waiting for transfers between devices: 224 us -> none  [shards(): preact, grad_act = lax.psum((part_pre, part_grad), 'col')]
    pallas_call x0 -> x2, Pallas kernels: none -> 128 us  [the longest x1 111 us: run_block(): pl.pallas_call(functools.partial(block_kernel, n_row, n_col, chunks), out...]
    dot_general x6 -> x0, matrix products: 71 us -> none  [the longest x1 14.4 us: shards(): lax.dot_general(grad_pre, weight_in, (((1,), (1,)), ((), ())), preferred_...]
    reduce_scatter x1, waiting for transfers between devices: 0.01 us -> 24.4 us  [shards(): lax.psum_scatter(part_back, 'row', scatter_dimension=0, tiled=True)]
    unnamed x5 -> x6, local copies, waits for them, and re-layouts: 24.7 us -> 3.87 us
    all_gather x2 -> x0, blocking collectives: 14.8 us -> none  [the longest x1 8.01 us: shards(): lax.all_gather(inputs, 'row', axis=0, tiled=True)]
    reduce_scatter x1, waiting for transfers between devices: 0.01 us -> 7.77 us  [shards(): lax.psum_scatter(part_out, 'row', scatter_dimension=0, tiled=True)]
    convert_element_type x1 -> x0, other arithmetic: 4.29 us -> none  [local_gelu(): return (value.astype(jnp.bfloat16), (grad_act * slope).astype(jnp.bfloat16))]
  transfers between devices with their start and end apart: 3 -> 2, of which waited for: 1 -> 2; matrix products, arithmetic and copies ran while one was open for 18% -> 1% of each run, Pallas kernels for 0% -> 9%
where the time goes in v1:
time: 183 us; the launch traced here: 182 us
  Pallas kernels  128 us (70%)
  waiting for transfers between devices  32.9 us (18%)
  between operations  14.1 us (8%)
  local copies, waits for them, and re-layouts  3.87 us (2%)
  other arithmetic  3.15 us (2%)
    pallas_call x1, Pallas kernels, run_block(): pl.pallas_call(functools.partial(block_kernel, n_row, n_col, chunks), out...  111 us
    reduce_scatter x1, waiting for transfers between devices, shards(): lax.psum_scatter(part_back, 'row', scatter_dimension=0, tiled=True)  24.4 us
    pallas_call x1, Pallas kernels, weight_grads(): pl.pallas_call(grads_kernel, grid=(chunks // per,), out_shape=(jax.ShapeD...  16.7 us
    reduce_scatter x1, waiting for transfers between devices, shards(): lax.psum_scatter(part_out, 'row', scatter_dimension=0, tiled=True)  7.77 us
    unnamed x6, local copies, waits for them, and re-layouts  3.87 us
  transfers between devices with their start and end apart: 2, of which 2 were waited for; matrix products, arithmetic and copies ran while one was open for 1% of the time, Pallas kernels for 9%

profile of v1, /device:TPU:1, one launch (start us, length us, event | category | flops | bytes accessed | tf_op | source)
XLA Modules:
  0.0 181.9 jit_solution(2351694083942416685)
XLA Ops:
  7.2 0.0 reduce-scatter.3.cloned.1.call-start
  7.2 111.2 %block.1 = (bf16[24,256,256]{2,1,0:T(8,128)(2,1)}, bf16[128,1536]{1,0:T(8,128)(2,1)}, bf16[128,1536]{1,0:T(8,128)(2,1)}, f32[128,1536]{1,0:T(8,128)}, f32[128,1536]{1,0:T(8,128)}) custom-call(bf16[32,1536]{1,0:T(8,128)(2,1)} %x_ref.1, bf16[32,1536]{1,0:T(8,128)(2,1)} %dy_ref.1, bf16[1536,6144]{1,0:T(8,128)(2,1)} %win_hbm.1, bf16[6144,1536]{1,0:T(8,128)(2,1)} %wout_hbm.1), custom_call_target="tpu_custom_call" | custom-call | flops 9663676416 | bytes 37748736 | tf_op jit(solution)/shard_map/block/pallas_call | solution.py:276
  118.4 0.0 reduce-scatter.3.cloned.1.call-update
  118.4 0.0 reduce-scatter.5.cloned.1.call-start
  118.5 0.7 reduce-scatter.5.cloned.1.call-update
  119.2 0.0 copy-start
  119.2 1.9 %copy-done = bf16[24,256,256]{2,1,0:T(8,128)(2,1)S(1)} copy-done((bf16[24,256,256]{2,1,0:T(8,128)(2,1)S(1)}, bf16[24,256,256]{2,1,0:T(8,128)(2,1)}, u32[]{:S(2)}) %copy-start) | copy-done | bytes 3145752
  121.1 0.0 copy-start.1
  121.1 1.0 copy-done.1
  122.1 0.0 copy-start.2
  122.1 1.0 copy-done.2
  123.0 16.7 %grads.1 = (bf16[1536,6144]{1,0:T(8,128)(2,1)}, bf16[6144,1536]{1,0:T(8,128)(2,1)}) custom-call(bf16[128,1536]{1,0:T(8,128)(2,1)S(1)} %copy-done.1, bf16[128,1536]{1,0:T(8,128)(2,1)S(1)} %copy-done.2, bf16[24,256,256]{2,1,0:T(8,128)(2,1)S(1)} %copy-done), custom_call_target="tpu_custom_call" | custom-call | flops 4831838208 | bytes 37748736 | tf_op jit(solution)/shard_map/grads/pallas_call | solution.py:343
  139.7 7.8 %reduce-scatter.3.cloned.1.call-done = f32[32,1536]{1,0:T(8,128)} async-done(((f32[128,1536]{1,0:T(8,128)}), f32[32,1536]{1,0:T(8,128)}) %reduce-scatter.3.cloned.1.call-update) | async-done | bytes 196624 | tf_op jit(solution)/shard_map/reduce_scatter | solution.py:375
  147.5 1.6 convert_element_type.6
  149.1 24.4 %reduce-scatter.5.cloned.1.call-done = f32[32,1536]{1,0:T(8,128)} async-done(((f32[128,1536]{1,0:T(8,128)}), f32[32,1536]{1,0:T(8,128)}) %reduce-scatter.5.cloned.1.call-update) | async-done | bytes 196624 | tf_op jit(solution)/shard_map/reduce_scatter | solution.py:376
  173.5 1.6 convert_element_type.7
Async XLA Ops:
  7.2 140.3 %reduce-scatter.3.cloned.1.call-start = ((), (), s32[]{:S(2)}) async-start(), calls=%async_computation.2 | async-start | bytes 983040 | tf_op jit(solution)/shard_map/reduce_scatter | solution.py:375
  118.4 55.1 %reduce-scatter.5.cloned.1.call-start = ((), (), s32[]{:S(2)}) async-start(), calls=%async_computation.3 | async-start | bytes 983040 | tf_op jit(solution)/shard_map/reduce_scatter | solution.py:376
  119.2 1.9 %copy-start = (bf16[24,256,256]{2,1,0:T(8,128)(2,1)S(1)}, bf16[24,256,256]{2,1,0:T(8,128)(2,1)}, u32[]{:S(2)}) copy-start(bf16[24,256,256]{2,1,0:T(8,128)(2,1)} %get-tuple-element.15.acts_ref) | copy-start | bytes 9437188
  121.1 1.0 copy-start.1
  122.1 1.0 copy-start.2
Sparse Core Ops, SparseCore 0:
  118.5 28.8 reduce-scatter.2
  150.2 23.2 reduce-scatter.4

commit v2 on v1

--- a/solution.py
+++ b/solution.py
@@ -30,9 +30,10 @@
 def block_kernel(
     n_row, n_col, chunks,
     x_ref, dy_ref, win_hbm, wout_hbm,
-    acts_hbm, xall_hbm, dyall_hbm, out_ref, back_ref,
-    xall, dyall, win, wout, local, outgoing, from_left, from_right, acts,
+    acts_hbm, xall_hbm, dyall_hbm, result_ref, gin_ref,
+    sums, core_in, chip_out, chip_in, xall, dyall, win, wout, local, outgoing, from_left, from_right, acts,
     w_sem, g_send, g_recv, rs_send, left_recv, right_recv, ag_send, ag_recv, save_sem, tok_sem,
+    core_send, core_recv, chip_send, chip_recv,
 ):
     row, col = lax.axis_index("row"), lax.axis_index("col")
     own = x_ref.shape[0]
@@ -98,8 +99,7 @@
     mine = pl.ds(pl.multiple_of(row * own, own), own)
     xall[mine, :] = x_ref[...]
     dyall[mine, :] = dy_ref[...]
-    out_ref[...] = jnp.zeros_like(out_ref)
-    back_ref[...] = jnp.zeros_like(back_ref)
+    sums[...] = jnp.zeros_like(sums)
     for which in range(2):
         for o in range(1, pairs):
             block = lax.rem(pair + pairs - o, pairs) * 2 + core
@@ -224,8 +224,8 @@
                 copy.start()
 
         save(k).start()
-        out_ref[...] += jnp.dot(acts[k, :tokens, :], wout[k], preferred_element_type=jnp.float32)
-        back_ref[...] += lax.dot_general(
+        sums[0] += jnp.dot(acts[k, :tokens, :], wout[k], preferred_element_type=jnp.float32)
+        sums[1] += lax.dot_general(
             acts[k, tokens:, :], win[k], NT, preferred_element_type=jnp.float32
         )
 
@@ -238,6 +238,37 @@
 
     lax.fori_loop(0, chunks + SPREAD, step, 0)
 
+    def rows_of(block):
+        return pl.ds(pl.multiple_of(block * own, own), own)
+
+    def to_core(which, o):
+        block = lax.rem(pair + o, pairs) * 2 + 1 - core
+        return pltpu.make_async_remote_copy(
+            src_ref=sums.at[which, rows_of(block)], dst_ref=core_in.at[which, o],
+            send_sem=core_send.at[which, o], recv_sem=core_recv.at[which, o],
+            device_id={"row": sibling}, device_id_type=MESH,
+        )
+
+    def to_chip(which, o):
+        return pltpu.make_async_remote_copy(
+            src_ref=chip_out.at[which, o], dst_ref=chip_in.at[which, o],
+            send_sem=chip_send.at[which, o], recv_sem=chip_recv.at[which, o],
+            device_id={"row": lax.rem(pair + o, pairs) * 2 + core}, device_id_type=MESH,
+        )
+
+    order = list(range(1, pairs)) + [0]
+    for o in order:
+        for which in range(2):
+            to_core(which, o).start()
+    for o in order[:-1]:
+        block = lax.rem(pair + o, pairs) * 2 + core
+        for which in range(2):
+            to_core(which, o).wait_recv()
+            chip_out[which, o] = (sums[which, rows_of(block), :] + core_in[which, o]).astype(
+                jnp.bfloat16
+            )
+            to_chip(which, o).start()
+
     def drain(k, carry):
         @pl.when(col < owner(k))
         def _():
@@ -261,6 +292,18 @@
     lax.fori_loop(0, chunks, drain, 0)
     for copy in keep:
         copy.wait()
+    for which, ref in ((0, result_ref), (1, gin_ref)):
+        to_core(which, 0).wait_recv()
+        total = sums[which, rows_of(row), :] + core_in[which, 0]
+        for o in range(1, pairs):
+            to_chip(which, o).wait_recv()
+            total += chip_in[which, o].astype(jnp.float32)
+        ref[...] = total.astype(jnp.bfloat16)
+    for which in range(2):
+        for o in order:
+            to_core(which, o).wait_send()
+        for o in order[:-1]:
+            to_chip(which, o).wait_send()
 
 
 def run_block(n_row, n_col, x, dy, w_in, w_out):
@@ -279,12 +322,16 @@
             jax.ShapeDtypeStruct(stack, bf),
             jax.ShapeDtypeStruct((tokens, depth), bf),
             jax.ShapeDtypeStruct((tokens, depth), bf),
-            jax.ShapeDtypeStruct((tokens, depth), f32),
-            jax.ShapeDtypeStruct((tokens, depth), f32),
+            jax.ShapeDtypeStruct((own, depth), bf),
+            jax.ShapeDtypeStruct((own, depth), bf),
         ),
         in_specs=[vmem, vmem, anywhere, anywhere],
         out_specs=(anywhere, anywhere, anywhere, vmem, vmem),
         scratch_shapes=[
+            pltpu.VMEM((2, tokens, depth), f32),
+            pltpu.VMEM((2, n_row // 2, own, depth), f32),
+            pltpu.VMEM((2, n_row // 2, own, depth), bf),
+            pltpu.VMEM((2, n_row // 2, own, depth), bf),
             pltpu.VMEM((tokens, depth), bf),
             pltpu.VMEM((tokens, depth), bf),
             pltpu.VMEM((chunks, depth, CHUNK), bf),
@@ -304,6 +351,10 @@
             dma((chunks,)),
             dma((chunks,)),
             dma((2,)),
+            dma((2, n_row // 2)),
+            dma((2, n_row // 2)),
+            dma((2, n_row // 2)),
+            dma((2, n_row // 2)),
         ],
         compiler_params=pltpu.CompilerParams(
             collective_id=0, has_side_effects=True, vmem_limit_bytes=60 * 2**20
@@ -357,7 +408,7 @@
             pl.BlockSpec((per * CHUNK, depth), lambda s: (s, 0)),
         ),
         scratch_shapes=[pltpu.VMEM((depth, tokens), bf)],
-        compiler_params=pltpu.CompilerParams(vmem_limit_bytes=40 * 2**20),
+        compiler_params=pltpu.CompilerParams(vmem_limit_bytes=60 * 2**20),
         cost_estimate=pl.CostEstimate(
             flops=4 * tokens * depth * hidden,
             bytes_accessed=4 * depth * hidden,
@@ -368,20 +419,11 @@
 
 
 def shards(n_row, n_col, inputs, upstream, weight_in, weight_out):
-    acts, x_all, dy_all, part_out, part_back = run_block(
+    acts, x_all, dy_all, result, grad_inputs = run_block(
         n_row, n_col, inputs, upstream, weight_in, weight_out
     )
-    summed_out, summed_back = (
-        lax.psum_scatter(part_out, "row", scatter_dimension=0, tiled=True),
-        lax.psum_scatter(part_back, "row", scatter_dimension=0, tiled=True),
-    )
     grad_weight_in, grad_weight_out = weight_grads(x_all, dy_all, acts)
-    return (
-        summed_out.astype(jnp.bfloat16),
-        summed_back.astype(jnp.bfloat16),
-        grad_weight_in,
-        grad_weight_out,
-    )
+    return result, grad_inputs, grad_weight_in, grad_weight_out
 
 
 def solution(mesh):

time: 183 us -> 146 us (0.80)
  waiting for transfers between devices: 32.9 us -> 0 us
  Pallas kernels: 128 us -> 142 us
  between operations: 14.1 us -> 0.64 us
  other arithmetic: 3.15 us -> 0 us
    reduce_scatter x2 -> x0, waiting for transfers between devices: 32.2 us -> none  [the longest x1 24.4 us: shards(): lax.psum_scatter(part_back, 'row', scatter_dimension=0, tiled=True)]
    pallas_call x1, Pallas kernels: 111 us -> 124 us  [run_block(): pl.pallas_call(functools.partial(block_kernel, n_row, n_col, chunks), out...]
    convert_element_type x2 -> x0, other arithmetic: 3.15 us -> none  [the longest x1 1.58 us: shards(): summed_out.astype(jnp.bfloat16)]
    unnamed x6 -> x2, local copies, waits for them, and re-layouts: 3.87 us -> 3.08 us
  transfers between devices with their start and end apart: 2 -> 0, of which waited for: 2 -> 0; matrix products, arithmetic and copies ran while one was open for 1% -> 0% of each run, Pallas kernels for 9% -> 0%
where the time goes in v2:
time: 146 us
  Pallas kernels  142 us (97%)
  local copies, waits for them, and re-layouts  3.08 us (2%)
    pallas_call x1, Pallas kernels, run_block(): pl.pallas_call(functools.partial(block_kernel, n_row, n_col, chunks), out...  124 us
    pallas_call x1, Pallas kernels, weight_grads(): pl.pallas_call(grads_kernel, grid=(chunks // per,), out_shape=(jax.ShapeD...  18 us
    unnamed x2, local copies, waits for them, and re-layouts  3.08 us

profile of v2, /device:TPU:1, one launch (start us, length us, event | category | flops | bytes accessed | tf_op | source)
XLA Modules:
  0.0 146.1 jit_solution(2802918744027805526)
XLA Ops:
  0.6 124.4 %block.1 = (bf16[24,256,256]{2,1,0:T(8,128)(2,1)}, bf16[128,1536]{1,0:T(8,128)(2,1)}, bf16[128,1536]{1,0:T(8,128)(2,1)}, bf16[32,1536]{1,0:T(8,128)(2,1)}, bf16[32,1536]{1,0:T(8,128)(2,1)}) custom-call(bf16[32,1536]{1,0:T(8,128)(2,1)} %x_ref.1, bf16[32,1536]{1,0:T(8,128)(2,1)} %dy_ref.1, bf16[1536,6144]{1,0:T(8,128)(2,1)} %win_hbm.1, bf16[6144,1536]{1,0:T(8,128)(2,1)} %wout_hbm.1), custom_call_target="tpu_custom_call" | custom-call | flops 9663676416 | bytes 37748736 | tf_op jit(solution)/shard_map/block/pallas_call | solution.py:319
  125.0 18.0 %grads.1 = (bf16[1536,6144]{1,0:T(8,128)(2,1)}, bf16[6144,1536]{1,0:T(8,128)(2,1)}) custom-call(bf16[128,1536]{1,0:T(8,128)(2,1)} %get-tuple-element.13.x_ref, bf16[128,1536]{1,0:T(8,128)(2,1)} %get-tuple-element.14.dy_ref, bf16[24,256,256]{2,1,0:T(8,128)(2,1)} %get-tuple-element.15.acts_ref), custom_call_target="tpu_custom_call" | custom-call | flops 4831838208 | bytes 37748736 | tf_op jit(solution)/shard_map/grads/pallas_call | solution.py:394
  143.0 1.5 %copy.10 = bf16[32,1536]{1,0:T(8,128)(2,1)} copy(bf16[32,1536]{1,0:T(8,128)(2,1)} %get-tuple-element.22) | data formatting | bytes 196608
  144.5 1.5 %copy.11 = bf16[32,1536]{1,0:T(8,128)(2,1)} copy(bf16[32,1536]{1,0:T(8,128)(2,1)} %get-tuple-element.23) | data formatting | bytes 196608

commit v3 on v2

--- a/solution.py
+++ b/solution.py
@@ -10,7 +10,7 @@
 
 gelu_c = math.sqrt(2.0 / math.pi)
 MESH = pl.DeviceIdType.MESH
-CHUNK = 256
+CHUNK = 512
 RING = 8
 RELAY, OWN, SPREAD = 1, 3, 6
 NT = (((1,), (1,)), ((), ()))

time: 146 us -> 141 us (0.966)
  Pallas kernels: 142 us -> 137 us
    pallas_call x1, Pallas kernels: 124 us -> 122 us  [run_block(): pl.pallas_call(functools.partial(block_kernel, n_row, n_col, chunks), out...]
    pallas_call x1, Pallas kernels: 18 us -> 15.5 us  [weight_grads(): pl.pallas_call(grads_kernel, grid=(chunks // per,), out_shape=(jax.ShapeD...]
where the time goes in v3:
time: 141 us
  Pallas kernels  137 us (97%)
  local copies, waits for them, and re-layouts  3.08 us (2%)
    pallas_call x1, Pallas kernels, run_block(): pl.pallas_call(functools.partial(block_kernel, n_row, n_col, chunks), out...  122 us
    pallas_call x1, Pallas kernels, weight_grads(): pl.pallas_call(grads_kernel, grid=(chunks // per,), out_shape=(jax.ShapeD...  15.5 us
    unnamed x2, local copies, waits for them, and re-layouts  3.08 us

profile of v3, /device:TPU:1, one launch (start us, length us, event | category | flops | bytes accessed | tf_op | source)
XLA Modules:
  0.0 140.7 jit_solution(8854971818747845867)
XLA Ops:
  0.6 121.5 %block.1 = (bf16[12,256,512]{2,1,0:T(8,128)(2,1)}, bf16[128,1536]{1,0:T(8,128)(2,1)}, bf16[128,1536]{1,0:T(8,128)(2,1)}, bf16[32,1536]{1,0:T(8,128)(2,1)}, bf16[32,1536]{1,0:T(8,128)(2,1)}) custom-call(bf16[32,1536]{1,0:T(8,128)(2,1)} %x_ref.1, bf16[32,1536]{1,0:T(8,128)(2,1)} %dy_ref.1, bf16[1536,6144]{1,0:T(8,128)(2,1)} %win_hbm.1, bf16[6144,1536]{1,0:T(8,128)(2,1)} %wout_hbm.1), custom_call_target="tpu_custom_call" | custom-call | flops 9663676416 | bytes 37748736 | tf_op jit(solution)/shard_map/block/pallas_call | solution.py:319
  122.2 15.5 %grads.1 = (bf16[1536,6144]{1,0:T(8,128)(2,1)}, bf16[6144,1536]{1,0:T(8,128)(2,1)}) custom-call(bf16[128,1536]{1,0:T(8,128)(2,1)} %get-tuple-element.13.x_ref, bf16[128,1536]{1,0:T(8,128)(2,1)} %get-tuple-element.14.dy_ref, bf16[12,256,512]{2,1,0:T(8,128)(2,1)} %get-tuple-element.15.acts_ref), custom_call_target="tpu_custom_call" | custom-call | flops 4831838208 | bytes 37748736 | tf_op jit(solution)/shard_map/grads/pallas_call | solution.py:394
  137.6 1.5 %copy.10 = bf16[32,1536]{1,0:T(8,128)(2,1)} copy(bf16[32,1536]{1,0:T(8,128)(2,1)} %get-tuple-element.22) | data formatting | bytes 196608
  139.2 1.5 %copy.11 = bf16[32,1536]{1,0:T(8,128)(2,1)} copy(bf16[32,1536]{1,0:T(8,128)(2,1)} %get-tuple-element.23) | data formatting | bytes 196608

commit v4 on v3

--- a/solution.py
+++ b/solution.py
@@ -12,7 +12,7 @@
 MESH = pl.DeviceIdType.MESH
 CHUNK = 512
 RING = 8
-RELAY, OWN, SPREAD = 1, 3, 6
+RELAY, OWN, SPREAD = 1, 2, 4
 NT = (((1,), (1,)), ((), ()))
 TN = (((0,), (0,)), ((), ()))
 

time: 141 us -> 136 us (0.965)
  Pallas kernels: 137 us -> 132 us
    pallas_call x1, Pallas kernels: 122 us -> 117 us  [run_block(): pl.pallas_call(functools.partial(block_kernel, n_row, n_col, chunks), out...]
where the time goes in v4:
time: 136 us
  Pallas kernels  132 us (97%)
  local copies, waits for them, and re-layouts  3.08 us (2%)
    pallas_call x1, Pallas kernels, run_block(): pl.pallas_call(functools.partial(block_kernel, n_row, n_col, chunks), out...  117 us
    pallas_call x1, Pallas kernels, weight_grads(): pl.pallas_call(grads_kernel, grid=(chunks // per,), out_shape=(jax.ShapeD...  15.5 us
    unnamed x2, local copies, waits for them, and re-layouts  3.08 us

profile of v4, /device:TPU:1, one launch (start us, length us, event | category | flops | bytes accessed | tf_op | source)
XLA Modules:
  0.0 136.0 jit_solution(14676567799989031522)
XLA Ops:
  0.6 116.9 %block.1 = (bf16[12,256,512]{2,1,0:T(8,128)(2,1)}, bf16[128,1536]{1,0:T(8,128)(2,1)}, bf16[128,1536]{1,0:T(8,128)(2,1)}, bf16[32,1536]{1,0:T(8,128)(2,1)}, bf16[32,1536]{1,0:T(8,128)(2,1)}) custom-call(bf16[32,1536]{1,0:T(8,128)(2,1)} %x_ref.1, bf16[32,1536]{1,0:T(8,128)(2,1)} %dy_ref.1, bf16[1536,6144]{1,0:T(8,128)(2,1)} %win_hbm.1, bf16[6144,1536]{1,0:T(8,128)(2,1)} %wout_hbm.1), custom_call_target="tpu_custom_call" | custom-call | flops 9663676416 | bytes 37748736 | tf_op jit(solution)/shard_map/block/pallas_call | solution.py:319
  117.5 15.5 %grads.1 = (bf16[1536,6144]{1,0:T(8,128)(2,1)}, bf16[6144,1536]{1,0:T(8,128)(2,1)}) custom-call(bf16[128,1536]{1,0:T(8,128)(2,1)} %get-tuple-element.13.x_ref, bf16[128,1536]{1,0:T(8,128)(2,1)} %get-tuple-element.14.dy_ref, bf16[12,256,512]{2,1,0:T(8,128)(2,1)} %get-tuple-element.15.acts_ref), custom_call_target="tpu_custom_call" | custom-call | flops 4831838208 | bytes 37748736 | tf_op jit(solution)/shard_map/grads/pallas_call | solution.py:394
  133.0 1.5 %copy.10 = bf16[32,1536]{1,0:T(8,128)(2,1)} copy(bf16[32,1536]{1,0:T(8,128)(2,1)} %get-tuple-element.22) | data formatting | bytes 196608
  134.5 1.5 %copy.11 = bf16[32,1536]{1,0:T(8,128)(2,1)} copy(bf16[32,1536]{1,0:T(8,128)(2,1)} %get-tuple-element.23) | data formatting | bytes 196608
